TPU v7x, 32 devices: a whole 2x2x4 slice. The times are simulated.
32 devices in a mesh: pair: 2 (over x), grow: 4 (over y, core), gcol: 4 (over z).
Axes of the slice: x: 2, y: 2, z: 4, core: 2. Of those that a mesh axis runs over, the one named last changes fastest.
Arguments:
- pair_elements: bfloat16 [1792, 8192], P('pair', ('grow', 'gcol')), may hold values from -0.75 to 0.75
- coulomb_root: float32 [8192], replicated, may hold values from 0.25 to 1
Outputs:
- factored: float32 [8192, 8192], P('grow', ('gcol', 'pair'))
All inputs are finite; a program needn't handle non-finite values.
Results may differ from a plain program's by a relative error of at most 0.0003.
Values may be sent and summed in bfloat16 or wider, within the bound.
A program may use at most 128 MiB of HBM per device.

v0:
```python
import jax
import jax.numpy as jnp
from jax import lax
from jax.sharding import PartitionSpec as P

PANEL = 512
PANELS = 2


def from_root(array, axis, root):
    mine = lax.axis_index(axis) == root
    return lax.psum(jnp.where(mine, array, jnp.zeros_like(array)), axis)


def body(pair_elements, coulomb_root):
    grid_total = coulomb_root.shape[0]
    tile_rows = grid_total // lax.axis_size("grow")
    tile_cols = grid_total // (lax.axis_size("gcol") * lax.axis_size("pair"))
    row_index = lax.axis_index("grow")
    col_index = lax.axis_index("gcol")
    gathered = lax.all_gather(pair_elements, ("grow", "gcol"), axis=1, tiled=True)
    row_block = lax.dynamic_slice_in_dim(gathered, row_index * tile_rows, tile_rows, 1)
    col_block = lax.dynamic_slice_in_dim(gathered, col_index * tile_rows, tile_rows, 1)
    flipped = lax.psum_scatter(
        lax.dot_general(
            col_block, row_block, (((0,), (0,)), ((), ())), preferred_element_type=jnp.float32
        ),
        "pair",
        scatter_dimension=0,
        tiled=True,
    )
    chi_tile = flipped.T
    row_base = row_index * tile_rows
    col_base = lax.axis_index(("gcol", "pair")) * tile_cols
    row_ids = row_base + jnp.arange(tile_rows, dtype=jnp.int32)[:, None]
    col_ids = col_base + jnp.arange(tile_cols, dtype=jnp.int32)[None, :]
    scale_rows = lax.dynamic_slice_in_dim(coulomb_root, row_base, tile_rows, 0)
    scale_cols = lax.dynamic_slice_in_dim(coulomb_root, col_base, tile_cols, 0)
    working = (
        jnp.where(row_ids == col_ids, 1.0, 0.0).astype(jnp.float32)
        + scale_rows[:, None] * chi_tile * scale_cols[None, :]
    )
    packed = jnp.zeros((tile_rows, tile_cols), jnp.float32)
    covered = jnp.zeros((tile_rows, tile_cols), bool)
    owner_width = min(PANEL, tile_cols)
    for step_index in range(PANELS):
        first = step_index * PANEL
        gathered_cols = []
        for owner in range(max(1, PANEL // tile_cols)):
            global_col = first + owner * owner_width
            local_col = global_col % tile_cols
            gathered_cols.append(
                from_root(
                    working[:, local_col : local_col + owner_width],
                    ("gcol", "pair"),
                    global_col // tile_cols,
                )
            )
        panel_cols = jnp.concatenate(gathered_cols, axis=1)
        local_row = first % tile_rows
        diag_block, panel_rows = (
            from_root(panel_cols[local_row : local_row + PANEL], "grow", first // tile_rows),
            from_root(working[local_row : local_row + PANEL], "grow", first // tile_rows),
        )
        factor = jnp.linalg.cholesky(diag_block)
        low_rows = lax.linalg.triangular_solve(
            factor, panel_cols, left_side=False, lower=True, transpose_a=True
        )
        low_cols = lax.linalg.triangular_solve(factor, panel_rows, left_side=True, lower=True)
        working = working - jnp.dot(low_rows, low_cols, precision=lax.Precision.HIGHEST)
        col_pos = col_ids - first
        in_cols = (col_pos >= 0) & (col_pos < PANEL) & (row_ids >= col_ids)
        col_vals = jnp.take(low_rows, jnp.clip(col_pos[0], 0, PANEL - 1), axis=1)
        row_pos = row_ids - first
        in_rows = (row_pos >= 0) & (row_pos < PANEL) & (col_ids > row_ids)
        row_vals = jnp.take(low_cols, jnp.clip(row_pos[:, 0], 0, PANEL - 1), axis=0)
        packed = packed + jnp.where(in_cols, col_vals, 0.0) + jnp.where(in_rows, row_vals, 0.0)
        covered = covered | in_cols | in_rows
    return jnp.where(covered, packed, working)


def solution(mesh):
    return jax.shard_map(
        body,
        mesh=mesh,
        in_specs=(P("pair", ("grow", "gcol")), P()),
        out_specs=P("grow", ("gcol", "pair")),
        check_vma=False,
    )
```

profile of v0, /device:TPU:4, one launch (start us, length us, event | category | flops | bytes accessed | tf_op | source)
XLA Modules:
  0.0 1212.9 jit_solution(15277184497236068876)
XLA Ops:
  7.3 120.4 %all-gather.2.cloned.1.call-done = bf16[896,8192]{1,0:T(8,128)(2,1)} async-done(((bf16[896,512]{1,0:T(8,128)(2,1)}), bf16[896,8192]{1,0:T(8,128)(2,1)}) %all-gather.2.cloned.1.call-update) | async-done | bytes 14680080 | tf_op jit(solution)/shard_map/all_gather | solution.py:21
  127.8 15.1 %fusion.11 = f32[2048,2048]{1,0:T(8,128)} fusion(bf16[896,8192]{1,0:T(8,128)(2,1)} %all-gather.2.cloned.1.call-done, s32[]{:T(128)} %select_n.87, s32[]{:T(128)S(6)} %select_n.88), kind=kOutput, calls=%fused_computation.29 | convolution fusion | flops 7516192768 | bytes 24117764 | tf_op jit(solution)/shard_map/dot_general | solution.py:25
  143.6 186.7 %reduce-scatter.2.cloned.1.call-done = f32[1024,2048]{1,0:T(8,128)} async-done(((f32[2048,2048]{1,0:T(8,128)}), f32[1024,2048]{1,0:T(8,128)}) %reduce-scatter.2.cloned.1.call-update) | async-done | bytes 8388624 | tf_op jit(solution)/shard_map/reduce_scatter | solution.py:24
  330.3 4.3 bitcast_add_fusion
  334.6 3.4 copy-done
  338.0 2.5 slice_select_fusion.1
  340.6 3.2 slice_select_fusion.3
  343.8 153.2 %all-reduce.8.cloned.1.call-done = f32[2048,512]{0,1:T(8,128)} async-done(((f32[2048,512]{0,1:T(8,128)}), f32[2048,512]{0,1:T(8,128)}) %all-reduce.8.cloned.1.call-update) | async-done | bytes 4194320 | tf_op jit(solution)/shard_map/psum | solution.py:12
  497.0 2.3 slice_select_fusion.5
  499.9 66.2 %all-reduce.14.cloned.1.call-done = (f32[512,1024]{0,1:T(8,128)}, f32[512,512]{0,1:T(8,128)}) async-done(((f32[512,1024]{0,1:T(8,128)}, f32[512,512]{0,1:T(8,128)}), (f32[512,1024]{0,1:T(8,128)}, f32[512,512]{0,1:T(8,128)})) %all-reduce.14.cloned.1.call-update) | async-done | bytes 3145744 | tf_op jit(solution)/shard_map/psum | solution.py:12
  566.1 1.6 copy.3
  569.1 11.7 cholesky.286
  581.0 9.8 custom-call.31
  591.5 11.7 cholesky.305
  603.3 10.0 custom-call.32
  613.9 11.7 cholesky.326
  625.6 9.8 custom-call.33
  636.1 11.7 cholesky.343
  652.8 7.7 while.8
  660.4 39.3 %custom-call.34 = f32[4,128,128]{1,2,0:T(8,128)S(1)} custom-call(f32[4,128,128]{2,1,0:T(8,128)S(1)} %get-tuple-element.38), custom_call_target="InvertDiagBlocksLowerTriangular" | custom-call | tf_op jit(solution)/shard_map/triangular_solve/custom-call.3 | solution.py:66
  699.8 1.8 fusion.70
  701.6 2.2 convolution_subtract_fusion.8
  704.5 1.8 convolution_subtract_fusion.6
  707.0 2.8 fusion.53
  709.8 1.5 fusion.106
  714.5 2.9 convolution_subtract_fusion.2
  718.6 3.7 fusion.29
  722.3 2.1 fusion.107
  724.4 17.2 %convolution_subtract_fusion = f32[2048,1024]{0,1:T(8,128)S(1)} fusion(f32[2048,1024]{0,1:T(8,128)S(1)} %bitcast.135, f32[128,1024]{1,0:T(8,128)} %fusion.106, f32[128,1024]{1,0:T(8,128)} %copy-done.9, f32[128,1024]{1,0:T(8,128)} %copy-done.7, f32[128,1024]{1,0:T(8,128)} %copy-done.4, f32[2048,128]{0,1:T(8,128)} %fusion.107, f32[2048,128]{0,1:T(8,128)} %copy-done.5, ...), kind=kOutput, calls=%fused_computation.28 | convolution fusion | flops 12891717632 | bytes 23068672 | tf_op jit(solution)/shard_map/dot_general | solution.py:70
  741.7 3.4 copy-done.1
  745.1 2.3 slice_select_fusion
  747.4 3.2 slice_select_fusion.2
  750.6 154.4 %all-reduce.10.cloned.1.call-done = f32[2048,512]{0,1:T(8,128)} async-done(((f32[2048,512]{0,1:T(8,128)}), f32[2048,512]{0,1:T(8,128)}) %all-reduce.10.cloned.1.call-update) | async-done | bytes 4194320 | tf_op jit(solution)/shard_map/psum | solution.py:12
  905.0 2.3 slice_select_fusion.4
  907.4 1.7 pad_maximum_fusion.2
  909.0 9.8 gather_fusion.1
  918.9 9.5 copy.4
  928.3 3.5 pad_maximum_fusion
  931.8 11.7 gather_fusion
  943.5 30.6 %all-reduce.12.cloned.1.call-done = (f32[512,1024]{0,1:T(8,128)}, f32[512,512]{0,1:T(8,128)}) async-done(((f32[512,1024]{0,1:T(8,128)}, f32[512,512]{0,1:T(8,128)}), (f32[512,1024]{0,1:T(8,128)}, f32[512,512]{0,1:T(8,128)})) %all-reduce.12.cloned.1.call-update) | async-done | bytes 3145744 | tf_op jit(solution)/shard_map/psum | solution.py:12
  974.1 1.6 copy.6
  977.1 11.7 cholesky.358
  989.0 9.8 custom-call.36
  999.5 11.7 cholesky.377
  1011.2 10.0 custom-call.37
  1021.9 11.7 cholesky.398
  1033.6 9.8 custom-call.38
  1044.0 11.7 cholesky.415
  1061.6 8.2 while.9
  1069.8 39.3 %custom-call.39 = f32[4,128,128]{1,2,0:T(8,128)S(1)} custom-call(f32[4,128,128]{2,1,0:T(8,128)S(1)} %get-tuple-element.40), custom_call_target="InvertDiagBlocksLowerTriangular" | custom-call | tf_op jit(solution)/shard_map/triangular_solve/custom-call.3 | solution.py:66
  1109.2 1.8 fusion.68
  1111.0 2.0 convolution_subtract_fusion.7
  1113.7 1.8 convolution_subtract_fusion.5
  1116.2 2.7 fusion.50
  1120.4 9.8 gather_fusion.3
  1130.2 9.6 copy.7
  1139.8 2.4 fusion.56
  1142.2 2.3 convolution_subtract_fusion.3
  1145.6 2.2 convolution_subtract_fusion.1
  1148.9 3.3 fusion.26
  1153.4 2.4 pad_maximum_fusion.1
  1155.8 11.2 gather_fusion.2
  1167.0 29.6 %fusion.8 = f32[2048,1024]{0,1:T(8,128)} fusion(f32[2048,1024]{0,1:T(8,128)} %copy.7, f32[1024,2048]{1,0:T(8,128)} %gather_fusion.2, f32[2048,1024]{0,1:T(8,128)} %copy.4, f32[1024,2048]{1,0:T(8,128)} %gather_fusion, f32[2048,1024]{0,1:T(8,128)} %copy-done.1, s32[2048]{0:T(1024)S(1)} %iota_add_fusion, pred[1024]{0:T(1024)(128)(4,1)S(1)} %get-tuple-element.98, ...), kind=kOutput, calls=%fused_computation.20 | convolution fusion | flops 12935757824 | bytes 56647680 | tf_op jit(solution)/shard_map/dot_general | solution.py:70
  1196.7 9.2 copy.9
  (146 shorter events, 42.0 us)
Async XLA Ops:
  6.5 121.2 %all-gather.2.cloned.1.call-start = ((), (), s32[]{:S(2)}) async-start(), calls=%async_computation.1 | async-start | bytes 15597568 | tf_op jit(solution)/shard_map/all_gather | solution.py:21
  7.3 323.0 %reduce-scatter.2.cloned.1.call-start = ((), (), s32[]{:S(2)}) async-start(), calls=%async_computation.2 | async-start | bytes 25165824 | tf_op jit(solution)/shard_map/reduce_scatter | solution.py:24
  142.8 0.8 copy-start.19
  142.8 187.5 %dynamic-slice-start = ((f32[8192]{0:T(1024)}, s32[]{:T(128)}), f32[2048]{0:T(1024)S(1)}, s32[]{:S(2)}) async-start(f32[8192]{0:T(1024)} %param.12, s32[]{:T(128)} %select_n.87), calls=%async_computation.9 | async-start | bytes 16896 | tf_op jit(solution)/shard_map/dynamic_slice | solution.py:37
  142.8 354.2 %all-reduce.8.cloned.1.call-start = ((), (), s32[]{:S(2)}) async-start(), calls=%async_computation.3 | async-start | bytes 8388608 | tf_op jit(solution)/shard_map/psum | solution.py:12
  334.6 3.4 copy-start
  340.5 225.6 %all-reduce.14.cloned.1.call-start = ((), (), s32[]{:S(2)}) async-start(), calls=%async_computation.6 | async-start | bytes 6291456 | tf_op jit(solution)/shard_map/psum | solution.py:12
  499.4 405.6 %all-reduce.10.cloned.1.call-start = ((), (), s32[]{:S(2)}) async-start(), calls=%async_computation.4 | async-start | bytes 8388608 | tf_op jit(solution)/shard_map/psum | solution.py:12
  660.4 51.9 %copy-start.14 = (f32[512,512]{1,0:T(8,128)}, f32[512,512]{1,0:T(8,128)S(1)}, u32[]{:S(2)}) copy-start(f32[512,512]{1,0:T(8,128)S(1)} %get-tuple-element.218) | copy-start | bytes 3145732
  699.8 4.8 copy-start.17
  701.6 8.2 copy-start.4
  703.9 7.4 copy-start.11
  704.5 7.8 copy-start.7
  707.0 6.4 copy-start.9
  713.4 11.0 slice-start
  714.5 9.9 copy-start.2
  717.5 6.9 slice-start.1
  718.6 3.7 copy-start.5
  741.7 3.4 copy-start.1
  747.4 226.7 %all-reduce.12.cloned.1.call-start = ((), (), s32[]{:S(2)}) async-start(), calls=%async_computation.5 | async-start | bytes 6291456 | tf_op jit(solution)/shard_map/psum | solution.py:12
  918.9 9.5 copy-start.3
  918.9 9.5 copy-start.6
  1069.8 49.1 %copy-start.13 = (f32[512,512]{1,0:T(8,128)}, f32[512,512]{1,0:T(8,128)S(1)}, u32[]{:S(2)}) copy-start(f32[512,512]{1,0:T(8,128)S(1)} %get-tuple-element.217) | copy-start | bytes 3145732
  1109.1 4.5 copy-start.16
  1116.2 3.4 copy-start.12
  1119.6 0.8 copy-start.18
  1139.7 5.9 copy-start.10
  1148.9 6.9 copy-start.8
  1153.4 2.5 copy-start.15
Sparse Core Ops, SparseCore 0:
  9.4 118.2 all-gather.1
  143.0 187.3 reduce-scatter.1
  340.6 156.3 all-reduce.7
  499.5 66.5 all-reduce.13
  747.5 157.4 all-reduce.9
  907.5 66.5 all-reduce.11
where the time goes:
time: 1220 us; the launch traced here: 1210 us
  waiting for transfers between devices  712 us (58%)
  other arithmetic  268 us (22%)
  matrix products  114 us (9%)
  local copies, waits for them, and re-layouts  98.1 us (8%)
  between operations  20 us (2%)
    psum x4, waiting for transfers between devices, from_root(): return lax.psum(jnp.where(mine, array, jnp.zeros_like(array)), axis)  404 us
    reduce_scatter x1, waiting for transfers between devices, body(): lax.psum_scatter(lax.dot_general(col_block, row_block, (((0,), (0,)), (()...  187 us
    another operation x29, other arithmetic, body(): factor = jnp.linalg.cholesky(diag_block)  158 us
    all_gather x1, waiting for transfers between devices, body(): lax.all_gather(pair_elements, ('grow', 'gcol'), axis=1, tiled=True)  120 us
    another operation x7, other arithmetic, body(): lax.linalg.triangular_solve(factor, panel_cols, left_side=False, lower=Tr...  85 us
    dot_general x2, matrix products, body(): jnp.dot(low_rows, low_cols, precision=lax.Precision.HIGHEST)  46.8 us
    gather x4, local copies, waits for them, and re-layouts, body(): row_vals = jnp.take(low_cols, jnp.clip(row_pos[:, 0], 0, PANEL - 1), axis=0)  38.7 us
    another operation x14, matrix products, body(): lax.linalg.triangular_solve(factor, panel_cols, left_side=False, lower=Tr...  26.6 us
  transfers between devices with their start and end apart: 6, of which 6 were waited for; matrix products, arithmetic and copies ran while one was open for 4% of the time, Pallas kernels for 0%

commit v1 on v0

v1 whole, which is shorter than its diff:
```python
import jax
import jax.numpy as jnp
from jax import lax
from jax.experimental import pallas as pl
from jax.experimental.pallas import tpu as pltpu
from jax.sharding import PartitionSpec as P

PANEL = 512
PANELS = 2
BASE = 128
FULL = lax.Precision.HIGHEST
HIGH = lax.Precision.HIGH


def gram(left, right):
    return lax.dot_general(
        left, right, (((0,), (0,)), ((), ())), preferred_element_type=jnp.float32
    )


def eliminate(block_ref, inverse_ref):
    tiles = [block_ref[at : at + 8, :] for at in range(0, BASE, 8)]
    lanes = lax.broadcasted_iota(jnp.int32, (8, BASE), 1)
    rows = lax.broadcasted_iota(jnp.int32, (8, BASE), 0)
    for step in range(BASE):
        tile, row = step // 8, step % 8
        own = tiles[tile]
        here = lanes == step
        pivot = jnp.broadcast_to(own[row : row + 1, :], (8, BASE))
        recip = 1.0 / jnp.broadcast_to(pivot[:, step : step + 1], (8, BASE))
        scaled = jnp.where(here, recip, pivot * recip)
        for at in range(tile, BASE // 8):
            if at == tile and row == 7:
                continue
            now = tiles[at]
            factor = jnp.broadcast_to(now[:, step : step + 1], (8, BASE))
            new = jnp.where(here, 0.0, now) - factor * scaled
            tiles[at] = jnp.where(rows > row, new, now) if at == tile else new
    for at, now in enumerate(tiles):
        diag = lanes == rows + 8 * at
        root = lax.rsqrt(jnp.sum(jnp.where(diag, now, 0.0), axis=1, keepdims=True))
        unit = jnp.where(diag, 1.0, jnp.where(lanes < rows + 8 * at, now, 0.0))
        inverse_ref[8 * at : 8 * at + 8, :] = unit * root


def small_inverse(block):
    return pl.pallas_call(
        eliminate,
        out_shape=jax.ShapeDtypeStruct((BASE, BASE), jnp.float32),
        in_specs=[pl.BlockSpec(memory_space=pltpu.VMEM)],
        out_specs=pl.BlockSpec(memory_space=pltpu.VMEM),
        cost_estimate=pl.CostEstimate(
            flops=BASE**3, bytes_accessed=8 * BASE**2, transcendentals=BASE
        ),
        name="eliminate",
    )(block)


def factor_inverse(block):
    size = block.shape[0]
    trailing = block
    inverse = None
    low = []
    for first in range(0, size, BASE):
        diag_inv = small_inverse(trailing[:BASE, :BASE])
        left = jnp.concatenate([c[first - at : first - at + BASE] for at, c in low], axis=1) if low else None
        if inverse is None:
            inverse = diag_inv
        else:
            below = -jnp.dot(
                diag_inv, jnp.dot(left, inverse, precision=FULL), precision=FULL
            )
            inverse = jnp.concatenate(
                [
                    jnp.pad(inverse, ((0, 0), (0, BASE))),
                    jnp.concatenate([below, diag_inv], axis=1),
                ],
                axis=0,
            )
        if first + BASE < size:
            column = lax.dot_general(
                trailing[BASE:, :BASE], diag_inv, (((1,), (1,)), ((), ())), precision=FULL
            )
            low.append((first + BASE, column))
            trailing = trailing[BASE:, BASE:] - lax.dot_general(
                column, column, (((1,), (1,)), ((), ())), precision=FULL
            )
    return inverse


def body(pair_elements, coulomb_root):
    grid_total = coulomb_root.shape[0]
    pairs, grows, gcols = (lax.axis_size(a) for a in ("pair", "grow", "gcol"))
    depth, width = pair_elements.shape
    total = depth * pairs
    tile_rows = grid_total // grows
    tile_cols = grid_total // (gcols * pairs)
    head = PANEL * PANELS
    row_index = lax.axis_index("grow")

    owners = head // width
    parts = grows * gcols
    spread = lax.all_to_all(
        pair_elements.reshape(parts, depth // parts, width), ("grow", "gcol"), 0, 0
    )
    head_el = lax.all_gather(spread[:owners], ("pair", "grow", "gcol"), axis=0)
    head_el = head_el.transpose(0, 2, 1, 3).reshape(total, head)
    head_el, pair_elements = lax.optimization_barrier((head_el, pair_elements))

    row_el = lax.all_gather(pair_elements, ("pair", "gcol"), axis=0)
    row_el = (
        row_el.reshape(pairs, gcols, depth, width)
        .transpose(0, 2, 1, 3)
        .reshape(total, tile_rows)
    )
    share = lax.dynamic_slice_in_dim(
        row_el, lax.axis_index("pair") * tile_cols, tile_cols, 1
    )
    col_el = lax.ppermute(
        share,
        ("grow", "gcol"),
        [(g * gcols + z, z * gcols + g) for g in range(grows) for z in range(gcols)],
    )

    row_base = row_index * tile_rows
    col_tile = lax.axis_index(("gcol", "pair"))
    col_base = col_tile * tile_cols
    scale_head = coulomb_root[:head]
    scale_rows = lax.dynamic_slice_in_dim(coulomb_root, row_base, tile_rows, 0)
    scale_cols = lax.dynamic_slice_in_dim(coulomb_root, col_base, tile_cols, 0)
    row_ids = row_base + jnp.arange(tile_rows, dtype=jnp.int32)[:, None]
    col_ids = col_base + jnp.arange(tile_cols, dtype=jnp.int32)[None, :]
    head_ids = jnp.arange(head, dtype=jnp.int32)

    def dielectric(left, right, left_scale, right_scale, left_ids, right_ids):
        return jnp.where(left_ids == right_ids, 1.0, 0.0).astype(jnp.float32) + (
            left_scale[:, None] * gram(left, right) * right_scale[None, :]
        )

    inverse = factor_inverse(
        dielectric(
            head_el, head_el, scale_head, scale_head, head_ids[:, None], head_ids[None, :]
        )
    )
    panel_cols = dielectric(
        row_el, head_el, scale_rows, scale_head, row_ids, head_ids[None, :]
    )
    panel_rows = dielectric(
        head_el, col_el, scale_head, scale_cols, head_ids[:, None], col_ids
    )
    low_rows = lax.dot_general(
        panel_cols, inverse, (((1,), (1,)), ((), ())), precision=HIGH
    )
    low_cols = jnp.dot(inverse, panel_rows, precision=HIGH)
    working = dielectric(
        row_el, col_el, scale_rows, scale_cols, row_ids, col_ids
    ) - jnp.dot(low_rows, low_cols, precision=HIGH)

    col_vals = lax.dynamic_slice_in_dim(
        low_rows, jnp.minimum(col_base, head - tile_cols), tile_cols, 1
    )
    row_vals = jnp.pad(low_cols, ((0, tile_rows - head), (0, 0)))
    in_cols = (col_ids < head) & (row_ids >= col_ids)
    in_rows = (row_ids < head) & (col_ids > row_ids)
    return jnp.where(in_cols, col_vals, jnp.where(in_rows, row_vals, working))


def solution(mesh):
    return jax.shard_map(
        body,
        mesh=mesh,
        in_specs=(P("pair", ("grow", "gcol")), P()),
        out_specs=P("grow", ("gcol", "pair")),
        check_vma=False,
    )
```

time: 1220 us -> 559 us (0.46)
  waiting for transfers between devices: 712 us -> 191 us
  other arithmetic: 268 us -> 0.7 us
  Pallas kernels: 0 us -> 150 us
  local copies, waits for them, and re-layouts: 98.1 us -> 41.4 us
  blocking collectives: 0 us -> 29.1 us
    psum x4 -> x0, waiting for transfers between devices: 404 us -> none  [from_root(): return lax.psum(jnp.where(mine, array, jnp.zeros_like(array)), axis)]
    another operation x38 -> x0, other arithmetic: 245 us -> none  [the longest x29 158 us: body(): factor = jnp.linalg.cholesky(diag_block)]
    reduce_scatter x1 -> x0, waiting for transfers between devices: 187 us -> none  [body(): lax.psum_scatter(lax.dot_general(col_block, row_block, (((0,), (0,)), (()...]
    pallas_call x0 -> x8, Pallas kernels: none -> 150 us  [small_inverse(): pl.pallas_call(eliminate, out_shape=jax.ShapeDtypeStruct((BASE, BASE), jn...]
    ppermute x0 -> x1, waiting for transfers between devices: none -> 131 us  [body(): lax.ppermute(share, ('grow', 'gcol'), [(g * gcols + z, z * gcols + g) for...]
    gather x6 -> x0, local copies, waits for them, and re-layouts: 61.5 us -> none  [the longest x4 38.7 us: body(): row_vals = jnp.take(low_cols, jnp.clip(row_pos[:, 0], 0, PANEL - 1), axis=0)]
    all_gather x1 -> x2, waiting for transfers between devices: 120 us -> 60.1 us  [the longest x1 60 us: body(): head_el = lax.all_gather(spread[:owners], ('pair', 'grow', 'gcol'), axis=0)]
    dot_general x3 -> x35, matrix products: 61.9 us -> 119 us  [the longest x4 39.5 us: gram(): lax.dot_general(left, right, (((0,), (0,)), ((), ())), preferred_element_...]
  transfers between devices with their start and end apart: 6 -> 3, of which waited for: 6 -> 2; matrix products, arithmetic and copies ran while one was open for 4% -> 15% of each run, Pallas kernels for 0% -> 27%
where the time goes in v1:
time: 559 us; the launch traced here: 549 us
  waiting for transfers between devices  191 us (34%)
  Pallas kernels  150 us (27%)
  matrix products  119 us (21%)
  local copies, waits for them, and re-layouts  41.4 us (7%)
  blocking collectives  29.1 us (5%)
  between operations  14.5 us (3%)
    pallas_call x8, Pallas kernels, small_inverse(): pl.pallas_call(eliminate, out_shape=jax.ShapeDtypeStruct((BASE, BASE), jn...  150 us
    ppermute x1, waiting for transfers between devices, body(): lax.ppermute(share, ('grow', 'gcol'), [(g * gcols + z, z * gcols + g) for...  131 us
    all_gather x1, waiting for transfers between devices, body(): head_el = lax.all_gather(spread[:owners], ('pair', 'grow', 'gcol'), axis=0)  60 us
    dot_general x4, matrix products, gram(): lax.dot_general(left, right, (((0,), (0,)), ((), ())), preferred_element_...  39.5 us
    all_to_all x1, blocking collectives, body(): lax.all_to_all(pair_elements.reshape(parts, depth // parts, width), ('gro...  29.1 us
    unnamed x54, local copies, waits for them, and re-layouts  18.4 us
    dot_general x1, matrix products, body(): lax.dot_general(panel_cols, inverse, (((1,), (1,)), ((), ())), precision=...  18.3 us
    dot_general x1, matrix products, body(): jnp.dot(low_rows, low_cols, precision=HIGH)  17.1 us
  transfers between devices with their start and end apart: 3, of which 2 were waited for; matrix products, arithmetic and copies ran while one was open for 15% of the time, Pallas kernels for 27%

profile of v1, /device:TPU:4, one launch (start us, length us, event | category | flops | bytes accessed | tf_op | source)
XLA Modules:
  0.0 549.0 jit_solution(1607412951082367917)
XLA Ops:
  6.5 29.1 %all_to_all.5 = bf16[16,56,512]{2,1,0:T(8,128)(2,1)S(1)} all-to-all(bf16[16,56,512]{2,1,0:T(8,128)(2,1)} %bitcast.71), channel_id=1, replica_groups=mesh['pair'=2,'grow'=4,'gcol'=4] {'grow','gcol'}, dimensions={0} | all-to-all | bytes 1835008 | tf_op jit(solution)/shard_map/all_to_all | solution.py:103
  35.7 0.7 slice.200
  36.4 60.0 %all-gather.5.cloned.1.call-done = bf16[64,56,512]{2,1,0:T(8,128)(2,1)} async-done(((bf16[2,56,512]{2,1,0:T(8,128)(2,1)}), bf16[64,56,512]{2,1,0:T(8,128)(2,1)}) %all-gather.5.cloned.1.call-update) | async-done | bytes 3670032 | tf_op jit(solution)/shard_map/all_gather | solution.py:106
  96.4 5.7 %copy.9 = bf16[32,56,2,512]{3,2,1,0:T(2,128)(2,1)S(1)} copy(bf16[32,56,2,512]{3,1,2,0:T(8,128)(2,1)} %bitcast.70) | data formatting | bytes 7340032 | tf_op jit(solution)/shard_map/transpose | solution.py:107
  102.1 2.9 copy.13
  105.2 7.4 %multiply_add_fusion = f32[1024,1024]{1,0:T(8,128)S(1)} fusion(bf16[1792,1024]{1,0:T(8,128)(2,1)} %bitcast.67, f32[1024]{0:T(1024)S(1)} %get-tuple-element.36), kind=kOutput, calls=%fused_computation.15 | convolution fusion | flops 3763339264 | bytes 7868416 | tf_op jit(solution)/shard_map/dot_general | solution.py:16
  112.6 2.0 copy-done.9
  114.6 0.6 slice.201.block_ref
  115.3 18.7 %eliminate.8 = f32[128,128]{1,0:T(8,128)} custom-call(f32[128,128]{1,0:T(8,128)} %slice.201.block_ref), custom_call_target="tpu_custom_call" | custom-call | flops 2097152 | bytes 131072 | tf_op jit(solution)/shard_map/eliminate/pallas_call | solution.py:47
  134.0 1.6 fusion.24
  135.6 5.2 slice_subtract_fusion
  140.8 0.6 slice.204.block_ref
  141.5 18.7 %eliminate.9 = f32[128,128]{1,0:T(8,128)} custom-call(f32[128,128]{1,0:T(8,128)} %slice.204.block_ref), custom_call_target="tpu_custom_call" | custom-call | flops 2097152 | bytes 131072 | tf_op jit(solution)/shard_map/eliminate/pallas_call | solution.py:47
  160.1 1.3 fusion.26
  161.5 2.1 slice_subtract_fusion.1
  163.6 1.4 copy-done.2
  165.0 0.6 slice.208.block_ref
  165.6 18.7 %eliminate.10 = f32[128,128]{1,0:T(8,128)} custom-call(f32[128,128]{1,0:T(8,128)} %slice.208.block_ref), custom_call_target="tpu_custom_call" | custom-call | flops 2097152 | bytes 131072 | tf_op jit(solution)/shard_map/eliminate/pallas_call | solution.py:47
  184.3 1.4 fusion.28
  185.7 3.1 slice_subtract_fusion.2
  188.9 0.6 slice.213.block_ref
  189.5 18.7 %eliminate.11 = f32[128,128]{1,0:T(8,128)} custom-call(f32[128,128]{1,0:T(8,128)} %slice.213.block_ref), custom_call_target="tpu_custom_call" | custom-call | flops 2097152 | bytes 131072 | tf_op jit(solution)/shard_map/eliminate/pallas_call | solution.py:47
  208.2 1.2 fusion.30
  209.4 1.1 convolution_subtract_fusion
  210.5 1.0 copy-done.8
  211.5 0.6 slice.219.block_ref
  212.1 18.7 %eliminate.12 = f32[128,128]{1,0:T(8,128)} custom-call(f32[128,128]{1,0:T(8,128)} %slice.219.block_ref), custom_call_target="tpu_custom_call" | custom-call | flops 2097152 | bytes 131072 | tf_op jit(solution)/shard_map/eliminate/pallas_call | solution.py:47
  230.8 1.3 fusion.40
  232.1 1.8 convolution_subtract_fusion.1
  233.9 0.6 slice.226.block_ref
  234.6 18.9 %eliminate.13 = f32[128,128]{1,0:T(8,128)} custom-call(f32[128,128]{1,0:T(8,128)} %slice.226.block_ref), custom_call_target="tpu_custom_call" | custom-call | flops 2097152 | bytes 131072 | tf_op jit(solution)/shard_map/eliminate/pallas_call | solution.py:47
  253.4 1.1 fusion.48
  254.6 0.4 convolution_subtract_fusion.2
  255.0 0.6 slice.234.block_ref
  255.6 18.7 %eliminate.14 = f32[128,128]{1,0:T(8,128)} custom-call(f32[128,128]{1,0:T(8,128)} %slice.234.block_ref), custom_call_target="tpu_custom_call" | custom-call | flops 2097152 | bytes 131072 | tf_op jit(solution)/shard_map/eliminate/pallas_call | solution.py:47
  274.3 0.7 slice_dynamic-update-slice_fusion.5
  275.0 0.7 slice_dynamic-update-slice_fusion.4
  275.6 0.7 slice_dynamic-update-slice_fusion.3
  276.3 0.6 slice_dynamic-update-slice_fusion.2
  276.9 0.6 slice_dynamic-update-slice_fusion.1
  277.6 0.6 slice_dynamic-update-slice_fusion
  278.2 0.8 copy-done.18
  279.0 1.7 constant_dynamic-update-slice_fusion
  280.7 0.9 convolution_subtract_fusion.3.block_ref
  281.6 18.7 %eliminate.15 = f32[128,128]{1,0:T(8,128)} custom-call(f32[128,128]{1,0:T(8,128)} %convolution_subtract_fusion.3.block_ref), custom_call_target="tpu_custom_call" | custom-call | flops 2097152 | bytes 131072 | tf_op jit(solution)/shard_map/eliminate/pallas_call | solution.py:47
  301.5 0.6 fusion.42
  302.5 0.7 fusion.32
  303.9 1.7 fusion.69
  305.7 0.4 convolution_negate_fusion.2
  306.3 1.4 fusion.70
  307.7 0.5 convolution_negate_fusion.1
  308.2 3.1 fusion.71
  311.3 11.8 %copy.10 = bf16[2,4,896,512]{3,1,2,0:T(4,128)(2,1)} copy(bf16[2,4,896,512]{3,2,1,0:T(8,128)(2,1)} %bitcast.66) | data formatting | bytes 14680064 | tf_op jit(solution)/shard_map/reshape | solution.py:112
  323.1 6.4 %copy.14 = bf16[224,8,4,512]{3,1,2,0:T(8,128)(2,1)S(1)} copy(bf16[224,8,4,512]{3,2,1,0:T(4,128)(2,1)} %bitcast.61) | data formatting | bytes 14680064
  329.5 0.4 constant_dynamic-slice_fusion
  330.0 3.5 collective-permute-start
  333.7 0.5 convolution_negate_fusion
  334.3 10.5 %fusion.73 = f32[2048,1024]{1,0:T(8,128)} fusion(bf16[1792,2048]{1,0:T(8,128)(2,1)S(1)} %bitcast.63, bf16[1792,1024]{1,0:T(8,128)(2,1)S(1)} %bitcast.68), kind=kOutput, calls=%fused_computation.129 | convolution fusion | flops 7516192768 | bytes 19398656 | tf_op jit(solution)/shard_map/dot_general | solution.py:16
  344.7 18.3 %fusion = f32[2048,1024]{1,0:T(8,128)} fusion(f32[2048,1024]{1,0:T(8,128)} %fusion.73, f32[1024]{0:T(1024)S(1)} %get-tuple-element.36, f32[2048]{0:T(1024)S(1)} %dynamic_slice.10, s32[2048]{0:T(1024)S(1)} %iota_add_fusion, f32[896,896]{1,0:T(8,128)S(1)} %select_maximum_fusion.1, f32[128,128]{1,0:T(8,128)S(1)} %copy-done.17, ...), kind=kOutput, calls=%fused_computation.1 | convolution fusion | flops 12899581952 | bytes 20533248 | tf_op jit(solution)/shard_map/dot_general | solution.py:151
  363.1 130.9 %collective-permute-done = bf16[1792,1024]{1,0:T(8,128)(2,1)S(1)} collective-permute-done((bf16[1792,1024]{1,0:T(8,128)(2,1)S(1)}, bf16[1792,1024]{1,0:T(8,128)(2,1)S(1)}, u32[]{:S(2)}, u32[]{:S(2)}) %collective-permute-start) | collective-permute-done | bytes 3670048 | tf_op jit(solution)/shard_map/ppermute | solution.py:119
  494.0 4.1 fusion.74
  498.1 8.9 %fusion.5 = f32[1024,1024]{1,0:T(8,128)} fusion(f32[1024,1024]{1,0:T(8,128)S(1)} %fusion.74, f32[896,896]{1,0:T(8,128)S(1)} %select_maximum_fusion.1, f32[128,128]{1,0:T(8,128)S(1)} %copy-done.17, f32[128,896]{1,0:T(8,128)S(1)} %convolution_negate_fusion, f32[1024]{0:T(1024)S(1)} %get-tuple-element.35, s32[1024]{0:T(1024)S(1)} %iota_add_fusion.1, ...), kind=kOutput, calls=%fused_computation.9 | convolution fusion | flops 6451888128 | bytes 12136448 | tf_op jit(solution)/shard_map/dot_general | solution.py:154
  507.0 17.1 %fusion.75 = f32[2048,1024]{1,0:T(8,128)} fusion(f32[2048,1024]{1,0:T(8,128)S(1)} %copy-done.22, f32[1024,1024]{1,0:T(8,128)} %fusion.5), kind=kOutput, calls=%fused_computation.131 | convolution fusion | flops 12884901888 | bytes 20971520 | tf_op jit(solution)/shard_map/dot_general | solution.py:157
  524.2 17.6 %select_select_fusion = f32[2048,1024]{1,0:T(8,128)} fusion(f32[2048,1024]{1,0:T(8,128)} %fusion, f32[2048,1024]{1,0:T(8,128)} %fusion.75, f32[1024,1024]{1,0:T(8,128)} %fusion.5, bf16[1792,2048]{1,0:T(8,128)(2,1)S(1)} %bitcast.64, bf16[1792,1024]{1,0:T(8,128)(2,1)} %copy-done.21, f32[1024]{0:T(1024)S(1)} %get-tuple-element.35, f32[2048]{0:T(1024)S(1)} %dynamic_slice.10, ...), kind=kOutput, calls=%fused_computation | convolution fusion | flops 7541358592 | bytes 40397824 | tf_op jit(solution)/shard_map/dot_general | solution.py:16
  (65 shorter events, 2.7 us)
Async XLA Ops:
  6.5 89.9 %all-gather.5.cloned.1.call-start = ((), (), s32[]{:S(2)}) async-start(), calls=%async_computation.1 | async-start | bytes 3784704 | tf_op jit(solution)/shard_map/all_gather | solution.py:106
  36.4 275.0 %all-gather.7.cloned.1.call-start = ((), (), s32[]{:S(2)}) async-start(), calls=%async_computation.2 | async-start | bytes 8257536 | tf_op jit(solution)/shard_map/all_gather | solution.py:110
  102.1 3.0 copy-start.20
  112.6 2.0 copy-start.9
  135.6 5.2 copy-start.3
  161.5 2.1 copy-start.5
  163.6 1.4 copy-start.2
  188.8 85.5 %copy-start.4 = (f32[896,128]{0,1:T(8,128)S(1)}, f32[896,128]{0,1:T(8,128)}, u32[]{:S(2)}) copy-start(f32[896,128]{0,1:T(8,128)} %copy-done.3) | copy-start | bytes 1376260
  209.4 65.6 %copy-start.6 = (f32[768,128]{0,1:T(8,128)S(1)}, f32[768,128]{0,1:T(8,128)}, u32[]{:S(2)}) copy-start(f32[768,128]{0,1:T(8,128)} %copy-done.5) | copy-start | bytes 1179652
  210.5 1.0 copy-start.8
  232.1 68.2 %copy-start.15 = (f32[128,128]{1,0:T(8,128)S(1)}, f32[128,128]{1,0:T(8,128)}, u32[]{:S(2)}) copy-start(f32[128,128]{1,0:T(8,128)} %eliminate.8) | copy-start | bytes 196612
  232.1 68.5 %copy-start.14 = (f32[128,128]{1,0:T(8,128)S(1)}, f32[128,128]{1,0:T(8,128)}, u32[]{:S(2)}) copy-start(f32[128,128]{1,0:T(8,128)} %eliminate.9) | copy-start | bytes 196612
  233.9 67.3 %copy-start.13 = (f32[128,128]{1,0:T(8,128)S(1)}, f32[128,128]{1,0:T(8,128)}, u32[]{:S(2)}) copy-start(f32[128,128]{1,0:T(8,128)} %eliminate.10) | copy-start | bytes 196612
  275.0 27.2 %copy-start.16 = (f32[128,128]{1,0:T(8,128)S(1)}, f32[128,128]{1,0:T(8,128)}, u32[]{:S(2)}) copy-start(f32[128,128]{1,0:T(8,128)} %eliminate.11) | copy-start | bytes 196612
  278.2 0.8 copy-start.18
  301.5 1.9 copy-start.12
  303.4 2.2 copy-start.10
  303.9 2.4 copy-start.19
  306.1 1.6 copy-start.11
  306.3 1.9 copy-start
  329.5 4.0 copy-start.1
  330.0 3.8 copy-start.17
  330.0 4.3 copy-start.7
  330.0 164.0 %collective-permute-start = (bf16[1792,1024]{1,0:T(8,128)(2,1)S(1)}, bf16[1792,1024]{1,0:T(8,128)(2,1)S(1)}, u32[]{:S(2)}, u32[]{:S(2)}) collective-permute-start(bf16[1792,1024]{1,0:T(8,128)(2,1)S(1)} %constant_dynamic-slice_fusion), channel_id=1, source_target_pairs={{0,0},{1,4},{2,8},{3,12},{4,1},{5,5},{6,9},{7,13},{8,2},{9,6},{10,... | collective-permute-start | bytes 11010056 | tf_op jit(solution)/shard_map/ppermute | solution.py:119
  494.0 4.1 copy-start.21
  498.1 8.9 %copy-start.22 = (f32[2048,1024]{1,0:T(8,128)S(1)}, f32[2048,1024]{1,0:T(8,128)}, u32[]{:S(2)}) copy-start(f32[2048,1024]{1,0:T(8,128)} %fusion) | copy-start | bytes 25165828
Sparse Core Ops, SparseCore 0:
  36.5 59.9 all-gather.4
  105.2 110.9 all-gather.6
